TPU v7x, 32 devices: a whole 2x2x4 slice. The times are simulated.
32 devices in a mesh: energy: 16 (over z, x, core), slab: 2 (over y).
Axes of the slice: x: 2, y: 2, z: 4, core: 2. Of those that a mesh axis runs over, the one named last changes fastest.
Arguments:
- green_blocks: bfloat16 [2, 12, 12, 256, 128], P(None, None, None, 'energy', 'slab'), may hold values from -6 to 6
- couplings: bfloat16 [12, 12, 2, 1024], P(None, None, 'slab', 'energy'), may hold values from -1.75 to 1.75
- band_weights: float32 [9, 2, 1024], P(None, 'slab', 'energy'), may hold values from 0.02 to 0.2
- neighbours: int32 [2, 1024], P('slab', 'energy'), may hold values from 0 to 127, as said below
- shifts: int32 [2, 1024], P('slab', 'energy'), may hold values from -32 to 32
Outputs:
- self_energy: bfloat16 [2, 12, 12, 256, 128], P(None, None, None, 'energy', 'slab')
Inputs may be any that keep to these rules, and one draw needn't show every extreme that they name: `neighbours`: the partner of each coupling of atom a lies within 4 atoms of a; partners of one atom may repeat.
All inputs are finite; a program needn't handle non-finite values.
Results may differ from a plain program's by a relative error of at most 0.0057.
Values may be sent and summed in bfloat16 or wider, within the bound.
A program may use at most 128 MiB of HBM per device.

v0:
```python
import functools

import jax
import jax.numpy as jnp
from jax import lax
from jax.experimental import pallas as pl
from jax.experimental.pallas import tpu as pltpu
from jax.sharding import PartitionSpec as P

ORB = 12
NBR = 16
BAND = 9
SHIFT = 32
HALO = 4
BLOCK = 2 * ORB * ORB
PAIR = ORB * ORB


def scatter_kernel(near_ref, shift_ref, left_ref, own_ref, right_ref, weight_ref, matrix_ref, out_ref,
                   green, spread_q, spread_r, total):
    per_dev = out_ref.shape[1] // BLOCK
    energies = out_ref.shape[0]
    half = energies // 2
    width = per_dev * BLOCK
    groups = lax.axis_size("energy")
    first_atom = (lax.axis_index("slab") * groups + lax.axis_index("energy")) * per_dev - HALO

    for place, ref in enumerate((left_ref, own_ref, right_ref)):
        green[place * width:(place + 1) * width, :] = ref[...].T

    lane_q = lax.broadcasted_iota(jnp.int32, (128, PAIR), 1)
    row_q = lax.broadcasted_iota(jnp.int32, (128, PAIR), 0)
    pick_q = (lane_q // ORB == row_q).astype(jnp.bfloat16)
    pick_r = (lane_q % ORB == row_q).astype(jnp.bfloat16)
    spread_q[...] = jnp.dot(matrix_ref[...], pick_q, preferred_element_type=jnp.float32).astype(jnp.bfloat16)
    spread_r[...] = jnp.dot(matrix_ref[...], pick_r, preferred_element_type=jnp.float32).astype(jnp.bfloat16)
    row_p = lax.broadcasted_iota(jnp.int32, (PAIR, 16), 0)
    lane_p = lax.broadcasted_iota(jnp.int32, (PAIR, 16), 1)
    pick_p = (row_p // ORB == lane_p).astype(jnp.bfloat16)
    pick_t = (row_p % ORB == lane_p).astype(jnp.bfloat16)
    below = lax.broadcasted_iota(jnp.int32, (half, half), 0) > lax.broadcasted_iota(jnp.int32, (half, half), 1)
    above = lax.broadcasted_iota(jnp.int32, (half, half), 0) < lax.broadcasted_iota(jnp.int32, (half, half), 1)

    sub = lax.broadcasted_iota(jnp.int32, (8, energies), 0)

    def atom(a, carry):
        total[...] = jnp.zeros_like(total)
        for k in range(NBR):
            index = a * NBR + k
            row = weight_ref[pl.ds(index, 1), :]
            turn = lax.rem(2 * energies - BAND // 2 - shift_ref[0, index], energies)
            tile = pltpu.roll(jnp.broadcast_to(row, (8, energies)), turn, 1)
            for step in (1, 2, 4):
                tile = jnp.where((sub & step) != 0, pltpu.roll(tile, step, 1), tile)
            band = jnp.concatenate([pltpu.roll(tile, 8 * b, 1) if b else tile for b in range(half // 8)], axis=0)
            near, far = band[:, :half], band[:, half:]
            near = near.astype(jnp.bfloat16)
            upper = jnp.where(below, far, 0.0).astype(jnp.bfloat16)
            lower = jnp.where(above, far, 0.0).astype(jnp.bfloat16)
            toeplitz = jnp.concatenate([
                jnp.concatenate([near, upper], axis=1),
                jnp.concatenate([lower, near], axis=1)], axis=0)
            partner = near_ref[0, index] - first_atom
            block = green[pl.ds(pl.multiple_of(partner * BLOCK, 32), BLOCK), :]
            banded = jnp.dot(block, toeplitz, preferred_element_type=jnp.float32).astype(jnp.bfloat16)
            rows = pl.ds(pl.multiple_of(index * 16, 16), 16)
            left = jnp.dot(pick_p, spread_q[rows, :], preferred_element_type=jnp.float32)
            right = jnp.dot(pick_t, spread_r[rows, :], preferred_element_type=jnp.float32)
            both = (left * right).astype(jnp.bfloat16)
            for c in range(2):
                part = slice(c * PAIR, (c + 1) * PAIR)
                total[part, :] += jnp.dot(both, banded[part], preferred_element_type=jnp.float32)
        return carry

    for a in range(per_dev):
        atom(a, 0)
        out_ref[:, a * BLOCK:(a + 1) * BLOCK] = total[...].T.astype(jnp.bfloat16)


def on_device(green_blocks, couplings, band_weights, neighbours, shifts):
    groups = lax.axis_size("energy")
    slabs = lax.axis_size("slab")
    local_e, slab_count = green_blocks.shape[3:]
    per_dev = slab_count // groups
    energies = local_e * groups
    width = per_dev * BLOCK
    pairs = per_dev * NBR
    assert per_dev == HALO
    group_pos = lax.axis_index("energy")

    sent = green_blocks.reshape(BLOCK, local_e, groups, per_dev).transpose(2, 1, 3, 0)
    sent = sent.reshape(groups, local_e, width)
    own = lax.all_to_all(sent, "energy", split_axis=0, concat_axis=0, tiled=True).reshape(energies, width)
    chain = [(s, g) for s in range(slabs) for g in range(groups)]
    rank = {pair: pair[1] * slabs + pair[0] for pair in chain}
    up = [(rank[chain[i]], rank[chain[i + 1]]) for i in range(len(chain) - 1)]
    down = [(j, i) for i, j in up]
    left = lax.ppermute(own, ("energy", "slab"), up)
    right = lax.ppermute(own, ("energy", "slab"), down)

    weight = jnp.pad(band_weights.reshape(BAND, pairs)[::-1].T, ((0, 0), (0, energies - BAND)))
    matrix = couplings.reshape(ORB, ORB, pairs).transpose(2, 0, 1)
    matrix = jnp.pad(matrix, ((0, 0), (0, 16 - ORB), (0, 128 - ORB))).reshape(pairs * 16, 128)
    vmem = pl.BlockSpec(memory_space=pltpu.VMEM)
    smem = pl.BlockSpec(memory_space=pltpu.SMEM)
    out = pl.pallas_call(
        scatter_kernel,
        out_shape=jax.ShapeDtypeStruct((energies, width), jnp.bfloat16),
        in_specs=[smem, smem, vmem, vmem, vmem, vmem, vmem],
        out_specs=vmem,
        scratch_shapes=[
            pltpu.VMEM((3 * width, energies), jnp.bfloat16),
            pltpu.VMEM((pairs * 16, PAIR), jnp.bfloat16),
            pltpu.VMEM((pairs * 16, PAIR), jnp.bfloat16),
            pltpu.VMEM((BLOCK, energies), jnp.float32),
        ],
        compiler_params=pltpu.CompilerParams(vmem_limit_bytes=40 * 1024 * 1024),
    )(neighbours, shifts, left, own, right, weight, matrix)
    back = lax.all_to_all(out.reshape(groups, local_e, width), "energy", split_axis=0, concat_axis=0, tiled=True)
    back = back.reshape(groups, local_e, per_dev, BLOCK).transpose(3, 1, 0, 2)
    return back.reshape(2, ORB, ORB, local_e, slab_count)


def solution(mesh):
    return jax.shard_map(
        on_device,
        mesh=mesh,
        in_specs=(
            P(None, None, None, "energy", "slab"),
            P(None, None, "slab", "energy"),
            P(None, "slab", "energy"),
            P("slab", "energy"),
            P("slab", "energy"),
        ),
        out_specs=P(None, None, None, "energy", "slab"),
        check_vma=False,
    )
```

profile of v0, /device:TPU:15, one launch (start us, length us, event | category | flops | bytes accessed | tf_op | source)
XLA Modules:
  0.0 140.2 jit_solution(16950896784193782812)
XLA Ops:
  0.0 15.1 %copy.14 = bf16[2,12,12,16,64]{2,1,0,3,4:T(8,128)(2,1)} copy(bf16[2,12,12,16,64]{4,3,2,1,0:T(8,128)(2,1)} %param.5) | data formatting | bytes 1179648 | tf_op args[0]
  15.1 0.0 copy-start.3
  15.1 0.0 copy-start.2
  15.1 0.0 copy-start
  15.1 0.0 copy-start.1
  15.1 12.1 %reshape.27 = bf16[288,16,16,4]{0,1,3,2:T(8,128)(2,1)S(1)} reshape(bf16[2,12,12,16,64]{2,1,0,3,4:T(8,128)(2,1)} %copy.14) | data formatting | bytes 1179648 | tf_op jit(solution)/shard_map/reshape | solution.py:91
  27.2 0.4 copy.15
  27.5 0.5 reshape.28
  28.1 21.5 %all_to_all.10 = bf16[16,16,1152]{2,1,0:T(8,128)(2,1)S(1)} all-to-all(bf16[16,16,1152]{2,1,0:T(8,128)(2,1)S(1)} %reshape.28), channel_id=1, replica_groups=mesh['energy'=16,'slab'=2] {'energy'}, dimensions={0} | all-to-all | bytes 1179648 | tf_op jit(solution)/shard_map/all_to_all | solution.py:93
  49.5 2.3 %collective-permute-start.1 = (bf16[256,1152]{1,0:T(8,128)(2,1)S(1)}, bf16[256,1152]{1,0:T(8,128)(2,1)S(1)}, u32[]{:S(2)}, u32[]{:S(2)}) collective-permute-start(bf16[256,1152]{1,0:T(8,128)(2,1)S(1)} %bitcast.16), channel_id=1, source_target_pairs={{2,0},{4,2},{6,4},{8,6},{10,8},{12,10},{14,12},{16,14},{18,16},{20... | collective-permute-start | bytes 1769480 | tf_op jit(solution)/shard_map/ppermute | solution.py:99
  51.8 4.3 %collective-permute-start = (bf16[256,1152]{1,0:T(8,128)(2,1)S(1)}, bf16[256,1152]{1,0:T(8,128)(2,1)S(1)}, u32[]{:S(2)}, u32[]{:S(2)}) collective-permute-start(bf16[256,1152]{1,0:T(8,128)(2,1)S(1)} %bitcast.17), channel_id=1, source_target_pairs={{0,2},{2,4},{4,6},{6,8},{8,10},{10,12},{12,14},{14,16},{16,18},{18... | collective-permute-start | bytes 1769480 | tf_op jit(solution)/shard_map/ppermute | solution.py:98
  56.2 0.0 copy-done.3
  56.2 0.1 copy.16
  56.3 0.1 rev.3
  56.3 0.0 copy-done.2
  56.3 0.3 copy.20
  56.7 0.1 pad.9.clone
  56.7 5.0 %collective-permute-done.1.right_ref = bf16[256,1152]{1,0:T(8,128)(2,1)S(1)} collective-permute-done((bf16[256,1152]{1,0:T(8,128)(2,1)S(1)}, bf16[256,1152]{1,0:T(8,128)(2,1)S(1)}, u32[]{:S(2)}, u32[]{:S(2)}) %collective-permute-start.1) | collective-permute-done | bytes 589856 | tf_op jit(solution)/shard_map/ppermute | solution.py:99
  61.7 1.1 collective-permute-done.left_ref
  62.8 0.0 copy-done
  62.8 0.0 copy-done.1
  62.8 21.2 %shard_map.55 = bf16[256,1152]{1,0:T(8,128)(2,1)S(1)} custom-call(s32[1,64]{1,0:T(1,128)S(1)} %copy-done, s32[1,64]{1,0:T(1,128)S(1)} %copy-done.1, bf16[256,1152]{1,0:T(8,128)(2,1)S(1)} %collective-permute-done.left_ref, bf16[256,1152]{1,0:T(8,128)(2,1)S(1)} %bitcast.18, bf16[256,1152]{1,0:T(8,128)(2,1)S(1)} %collective-permute-done.1.right_ref, ...), custom_call_target="tpu_custom_call" | custom-call | tf_op jit(solution)/shard_map/pallas_call | solution.py:106
  84.1 27.2 %all_to_all.11 = bf16[16,16,1152]{2,1,0:T(8,128)(2,1)S(1)} all-to-all(bf16[16,16,1152]{2,1,0:T(8,128)(2,1)S(1)} %bitcast.19), channel_id=1, replica_groups=mesh['energy'=16,'slab'=2] {'energy'}, dimensions={0} | all-to-all | bytes 1179648 | tf_op jit(solution)/shard_map/all_to_all | solution.py:119
  111.3 0.7 reshape.34
  112.0 0.1 copy.18
  112.1 15.9 %reshape.35 = bf16[2,12,12,16,64]{2,1,0,3,4:T(8,128)(2,1)} reshape(bf16[288,16,16,4]{0,1,3,2:T(8,128)(2,1)S(1)} %copy.18) | data formatting | bytes 1179648 | tf_op jit(solution)/shard_map/reshape | solution.py:121
  128.0 12.3 %copy.19 = bf16[2,12,12,16,64]{4,3,2,1,0:T(8,128)(2,1)} copy(bf16[2,12,12,16,64]{2,1,0,3,4:T(8,128)(2,1)} %reshape.35) | data formatting | bytes 1179648 | tf_op jit(solution)/shard_map/reshape | solution.py:121
  (1 shorter events, 0.0 us)
Async XLA Ops:
  15.1 41.1 %copy-start.3 = (f32[9,1,64]{2,1,0:T(1,128)S(1)}, f32[9,1,64]{2,1,0:T(1,128)}, u32[]{:S(2)}) copy-start(f32[9,1,64]{2,1,0:T(1,128)} %param.7) | copy-start | bytes 6916
  15.1 41.3 %copy-start.2 = (bf16[12,12,1,64]{3,1,2,0:T(8,128)(2,1)S(1)}, bf16[12,12,1,64]{3,1,2,0:T(8,128)(2,1)}, u32[]{:S(2)}) copy-start(bf16[12,12,1,64]{3,1,2,0:T(8,128)(2,1)} %param.6) | copy-start | bytes 55300
  15.1 47.8 %copy-start = (s32[1,64]{1,0:T(1,128)S(1)}, s32[1,64]{1,0:T(1,128)}, u32[]{:S(2)}) copy-start(s32[1,64]{1,0:T(1,128)} %near_ref.1) | copy-start | bytes 772
  15.1 47.8 %copy-start.1 = (s32[1,64]{1,0:T(1,128)S(1)}, s32[1,64]{1,0:T(1,128)}, u32[]{:S(2)}) copy-start(s32[1,64]{1,0:T(1,128)} %shift_ref.1) | copy-start | bytes 772
  49.5 12.2 %collective-permute-start.1 = (bf16[256,1152]{1,0:T(8,128)(2,1)S(1)}, bf16[256,1152]{1,0:T(8,128)(2,1)S(1)}, u32[]{:S(2)}, u32[]{:S(2)}) collective-permute-start(bf16[256,1152]{1,0:T(8,128)(2,1)S(1)} %bitcast.16), channel_id=1, source_target_pairs={{2,0},{4,2},{6,4},{8,6},{10,8},{12,10},{14,12},{16,14},{18,16},{20... | collective-permute-start | bytes 1769480 | tf_op jit(solution)/shard_map/ppermute | solution.py:99
  51.8 11.0 %collective-permute-start = (bf16[256,1152]{1,0:T(8,128)(2,1)S(1)}, bf16[256,1152]{1,0:T(8,128)(2,1)S(1)}, u32[]{:S(2)}, u32[]{:S(2)}) collective-permute-start(bf16[256,1152]{1,0:T(8,128)(2,1)S(1)} %bitcast.17), channel_id=1, source_target_pairs={{0,2},{2,4},{4,6},{6,8},{8,10},{10,12},{12,14},{14,16},{16,18},{18... | collective-permute-start | bytes 1769480 | tf_op jit(solution)/shard_map/ppermute | solution.py:98
where the time goes:
time: 143 us; the launch traced here: 140 us
  local copies, waits for them, and re-layouts  57.5 us (40%)
  blocking collectives  48.7 us (34%)
  Pallas kernels  21.2 us (15%)
  starting transfers between devices  6.63 us (5%)
  waiting for transfers between devices  6.11 us (4%)
    reshape x2, local copies, waits for them, and re-layouts, on_device(): return back.reshape(2, ORB, ORB, local_e, slab_count)  28.1 us
    all_to_all x1, blocking collectives, on_device(): lax.all_to_all(out.reshape(groups, local_e, width), 'energy', split_axis=...  27.2 us
    all_to_all x1, blocking collectives, on_device(): lax.all_to_all(sent, 'energy', split_axis=0, concat_axis=0, tiled=True)  21.5 us
    pallas_call x1, Pallas kernels, on_device(): pl.pallas_call(scatter_kernel, out_shape=jax.ShapeDtypeStruct((energies,...  21.2 us
    unnamed x11, local copies, waits for them, and re-layouts  15.5 us
    reshape x1, local copies, waits for them, and re-layouts, on_device(): green_blocks.reshape(BLOCK, local_e, groups, per_dev).transpose(2, 1, 3, 0)  12.1 us
    ppermute x1, waiting for transfers between devices, on_device(): right = lax.ppermute(own, ('energy', 'slab'), down)  4.98 us
    ppermute x1, starting transfers between devices, on_device(): left = lax.ppermute(own, ('energy', 'slab'), up)  4.34 us
  transfers between devices with their start and end apart: 2, of which 2 were waited for; matrix products, arithmetic and copies ran while one was open for 0% of the time, Pallas kernels for 0%

commit v1 on v0

--- a/solution.py
+++ b/solution.py
@@ -14,6 +14,95 @@
 HALO = 4
 BLOCK = 2 * ORB * ORB
 PAIR = ORB * ORB
+
+
+MESH = pl.DeviceIdType.MESH
+
+
+def order(groups, per_dev):
+    count = groups * per_dev
+    row = lax.broadcasted_iota(jnp.int32, (count, count), 0)
+    atom = lax.broadcasted_iota(jnp.int32, (count, count), 1)
+    return (atom == (row % groups) * per_dev + row // groups).astype(jnp.bfloat16)
+
+
+def pack_kernel(groups, per_dev, x_ref, sent, wide, packed):
+    local_e = sent.shape[1]
+    tiles = wide.shape[0]
+    count = x_ref.shape[1]
+    lanes = min(count, 128)
+    if lanes < 128:
+        wide[...] = jnp.zeros_like(wide)
+    for j in range(tiles):
+        wide[j, :x_ref.shape[0], :lanes] = x_ref[:, j * 128:j * 128 + lanes].astype(jnp.float32)
+    pick = order(groups, per_dev)
+    for e in range(local_e):
+        rows = jnp.concatenate([wide[j, pl.ds(e, BLOCK, stride=local_e), :] for j in range(tiles)], axis=1)
+        rows = rows[:, :count].astype(jnp.bfloat16)
+        turned = lax.dot_general(pick, rows, (((1,), (1,)), ((), ())), preferred_element_type=jnp.float32)
+        flat = jnp.concatenate([turned[i * groups:(i + 1) * groups] for i in range(per_dev)], axis=1)
+        for j in range(packed.shape[0]):
+            packed[j, pl.ds(e, groups, stride=local_e), :] = flat[:, j * 128:(j + 1) * 128]
+    for g in range(groups):
+        for j in range(packed.shape[0]):
+            sent[g, :, j * 128:(j + 1) * 128] = packed[j, g * local_e:(g + 1) * local_e, :].astype(jnp.bfloat16)
+
+
+def gather_kernel(groups, x_ref, landed, send_sem, recv_sem):
+    me, slab = lax.axis_index("energy"), lax.axis_index("slab")
+    barrier = pltpu.get_barrier_semaphore()
+
+    def hello(step, carry):
+        pl.semaphore_signal(barrier, inc=1, device_id=(lax.rem(me + step, groups), slab), device_id_type=MESH)
+        return carry
+
+    lax.fori_loop(1, groups, hello, 0)
+    pl.semaphore_wait(barrier, groups - 1)
+
+    def outgoing(step):
+        to = lax.rem(me + step, groups)
+        return pltpu.make_async_remote_copy(
+            src_ref=x_ref.at[to], dst_ref=landed.at[me], send_sem=send_sem.at[step], recv_sem=recv_sem.at[step],
+            device_id=(to, slab), device_id_type=MESH)
+
+    def incoming(step):
+        source = lax.rem(me - step + groups, groups)
+        return pltpu.make_async_remote_copy(
+            src_ref=x_ref.at[source], dst_ref=landed.at[source], send_sem=send_sem.at[step],
+            recv_sem=recv_sem.at[step], device_id=(source, slab), device_id_type=MESH)
+
+    def start(step, carry):
+        outgoing(step).start()
+        return carry
+
+    def finish(step, carry):
+        incoming(step).wait_recv()
+        outgoing(step).wait_send()
+        return carry
+
+    lax.fori_loop(1, groups, start, 0)
+    landed[me] = x_ref[me]
+    lax.fori_loop(1, groups, finish, 0)
+
+
+def unpack_kernel(groups, per_dev, landed, out_ref, wide, tall):
+    local_e = landed.shape[1]
+    lanes = min(out_ref.shape[1], 128)
+    for g in range(groups):
+        for j in range(wide.shape[0]):
+            wide[j, g * local_e:(g + 1) * local_e, :] = landed[g, :, j * 128:(j + 1) * 128].astype(jnp.float32)
+    pick = order(groups, per_dev)
+    for e in range(local_e):
+        rows = jnp.concatenate(
+            [wide[j, pl.ds(e, groups, stride=local_e), :] for j in range(wide.shape[0])], axis=1)
+        stack = jnp.concatenate([rows[:, i * BLOCK:(i + 1) * BLOCK] for i in range(per_dev)], axis=0)
+        turned = jnp.dot(stack.T.astype(jnp.bfloat16), pick, preferred_element_type=jnp.float32)
+        if lanes < 128:
+            turned = jnp.concatenate([turned, jnp.zeros((BLOCK, 128 - lanes), jnp.float32)], axis=1)
+        for j in range(tall.shape[0]):
+            tall[j, pl.ds(e, BLOCK, stride=local_e), :] = turned[:, j * 128:(j + 1) * 128]
+    for j in range(tall.shape[0]):
+        out_ref[:, j * 128:j * 128 + lanes] = tall[j, :out_ref.shape[0], :lanes].astype(jnp.bfloat16)
 
 
 def scatter_kernel(near_ref, shift_ref, left_ref, own_ref, right_ref, weight_ref, matrix_ref, out_ref,
@@ -60,7 +149,7 @@
             toeplitz = jnp.concatenate([
                 jnp.concatenate([near, upper], axis=1),
                 jnp.concatenate([lower, near], axis=1)], axis=0)
-            partner = near_ref[0, index] - first_atom
+            partner = jnp.clip(near_ref[0, index] - first_atom, 0, 3 * per_dev - 1)
             block = green[pl.ds(pl.multiple_of(partner * BLOCK, 32), BLOCK), :]
             banded = jnp.dot(block, toeplitz, preferred_element_type=jnp.float32).astype(jnp.bfloat16)
             rows = pl.ds(pl.multiple_of(index * 16, 16), 16)
@@ -86,23 +175,40 @@
     width = per_dev * BLOCK
     pairs = per_dev * NBR
     assert per_dev == HALO
-    group_pos = lax.axis_index("energy")
-
-    sent = green_blocks.reshape(BLOCK, local_e, groups, per_dev).transpose(2, 1, 3, 0)
-    sent = sent.reshape(groups, local_e, width)
-    own = lax.all_to_all(sent, "energy", split_axis=0, concat_axis=0, tiled=True).reshape(energies, width)
-    chain = [(s, g) for s in range(slabs) for g in range(groups)]
-    rank = {pair: pair[1] * slabs + pair[0] for pair in chain}
-    up = [(rank[chain[i]], rank[chain[i + 1]]) for i in range(len(chain) - 1)]
-    down = [(j, i) for i, j in up]
+    vmem = pl.BlockSpec(memory_space=pltpu.VMEM)
+    smem = pl.BlockSpec(memory_space=pltpu.SMEM)
+    blocks = jax.ShapeDtypeStruct((groups, local_e, width), jnp.bfloat16)
+    wide = pltpu.VMEM((pl.cdiv(slab_count, 128), BLOCK * local_e, 128), jnp.float32)
+    packed = pltpu.VMEM((width // 128, energies, 128), jnp.float32)
+    room = pltpu.CompilerParams(vmem_limit_bytes=32 * 1024 * 1024)
+    sent = pl.pallas_call(
+        functools.partial(pack_kernel, groups, per_dev),
+        out_shape=blocks, in_specs=[vmem], out_specs=vmem,
+        scratch_shapes=[wide, packed], compiler_params=room,
+    )(green_blocks.reshape(BLOCK * local_e, slab_count))
+    def exchanged(value, number):
+        return pl.pallas_call(
+            functools.partial(gather_kernel, groups),
+            out_shape=blocks,
+            in_specs=[vmem],
+            out_specs=vmem,
+            scratch_shapes=[
+                pltpu.SemaphoreType.DMA((groups,)),
+                pltpu.SemaphoreType.DMA((groups,)),
+            ],
+            compiler_params=pltpu.CompilerParams(
+                collective_id=number, has_side_effects=True, vmem_limit_bytes=32 * 1024 * 1024),
+        )(value)
+
+    own = exchanged(sent, 0).reshape(energies, width)
+    chain = [g * slabs + s for s in range(slabs) for g in range(groups)]
+    up = list(zip(chain[:-1], chain[1:]))
     left = lax.ppermute(own, ("energy", "slab"), up)
-    right = lax.ppermute(own, ("energy", "slab"), down)
+    right = lax.ppermute(own, ("energy", "slab"), [(j, i) for i, j in up])
 
     weight = jnp.pad(band_weights.reshape(BAND, pairs)[::-1].T, ((0, 0), (0, energies - BAND)))
     matrix = couplings.reshape(ORB, ORB, pairs).transpose(2, 0, 1)
     matrix = jnp.pad(matrix, ((0, 0), (0, 16 - ORB), (0, 128 - ORB))).reshape(pairs * 16, 128)
-    vmem = pl.BlockSpec(memory_space=pltpu.VMEM)
-    smem = pl.BlockSpec(memory_space=pltpu.SMEM)
     out = pl.pallas_call(
         scatter_kernel,
         out_shape=jax.ShapeDtypeStruct((energies, width), jnp.bfloat16),
@@ -116,8 +222,13 @@
         ],
         compiler_params=pltpu.CompilerParams(vmem_limit_bytes=40 * 1024 * 1024),
     )(neighbours, shifts, left, own, right, weight, matrix)
-    back = lax.all_to_all(out.reshape(groups, local_e, width), "energy", split_axis=0, concat_axis=0, tiled=True)
-    back = back.reshape(groups, local_e, per_dev, BLOCK).transpose(3, 1, 0, 2)
+    landed = exchanged(out.reshape(groups, local_e, width), 1)
+    back = pl.pallas_call(
+        functools.partial(unpack_kernel, groups, per_dev),
+        out_shape=jax.ShapeDtypeStruct((BLOCK * local_e, slab_count), jnp.bfloat16),
+        in_specs=[vmem], out_specs=vmem,
+        scratch_shapes=[packed, wide], compiler_params=room,
+    )(landed)
     return back.reshape(2, ORB, ORB, local_e, slab_count)
 
 

time: 143 us -> 82.2 us (0.57); the launches traced: 140 us -> 82 us
  local copies, waits for them, and re-layouts: 57.5 us -> 1.82 us
  blocking collectives: 48.7 us -> 0 us
  Pallas kernels: 21.2 us -> 67.3 us
    all_to_all x2 -> x0, blocking collectives: 48.7 us -> none  [the longest x1 27.2 us: on_device(): lax.all_to_all(out.reshape(groups, local_e, width), 'energy', split_axis=...]
    pallas_call x0 -> x4, Pallas kernels: none -> 46.1 us  [the longest x2 41.8 us: exchanged(): pl.pallas_call(functools.partial(gather_kernel, groups), out_shape=blocks...]
    reshape x5 -> x0, local copies, waits for them, and re-layouts: 41.4 us -> none  [the longest x2 28.1 us: on_device(): return back.reshape(2, ORB, ORB, local_e, slab_count)]
    unnamed x11 -> x12, local copies, waits for them, and re-layouts: 15.5 us -> 1.67 us
  transfers between devices with their start and end apart: 2 -> 2, of which waited for: 2 -> 2; matrix products, arithmetic and copies ran while one was open for 0% -> 1% of each run, Pallas kernels for 0% -> 0%
where the time goes in v1:
time: 82.2 us; the launch traced here: 82 us
  Pallas kernels  67.3 us (82%)
  starting transfers between devices  6.46 us (8%)
  waiting for transfers between devices  6.29 us (8%)
  local copies, waits for them, and re-layouts  1.82 us (2%)
    pallas_call x2, Pallas kernels, exchanged(): pl.pallas_call(functools.partial(gather_kernel, groups), out_shape=blocks...  41.8 us
    pallas_call x1, Pallas kernels, on_device(): pl.pallas_call(scatter_kernel, out_shape=jax.ShapeDtypeStruct((energies,...  21.2 us
    ppermute x1, waiting for transfers between devices, on_device(): right = lax.ppermute(own, ('energy', 'slab'), [(j, i) for i, j in up])  5.16 us
    ppermute x1, starting transfers between devices, on_device(): left = lax.ppermute(own, ('energy', 'slab'), up)  4.49 us
    pallas_call x1, Pallas kernels, on_device(): pl.pallas_call(functools.partial(unpack_kernel, groups, per_dev), out_sha...  2.74 us
    ppermute x1, starting transfers between devices, on_device(): right = lax.ppermute(own, ('energy', 'slab'), [(j, i) for i, j in up])  1.97 us
    unnamed x12, local copies, waits for them, and re-layouts  1.67 us
  transfers between devices with their start and end apart: 2, of which 2 were waited for; matrix products, arithmetic and copies ran while one was open for 1% of the time, Pallas kernels for 0%

profile of v1, /device:TPU:15, one launch (start us, length us, event | category | flops | bytes accessed | tf_op | source)
XLA Modules:
  0.0 82.0 jit_solution(6831175427100853794)
XLA Ops:
  0.0 0.0 copy-start
  0.0 1.3 %copy-done = bf16[2,12,12,16,64]{4,3,2,1,0:T(8,128)(2,1)S(1)} copy-done((bf16[2,12,12,16,64]{4,3,2,1,0:T(8,128)(2,1)S(1)}, bf16[2,12,12,16,64]{4,3,2,1,0:T(8,128)(2,1)}, u32[]{:S(2)}) %copy-start) | copy-done | bytes 589848
  1.3 0.0 copy-start.4
  1.3 0.0 copy-start.3
  1.3 1.6 %shard_map.55.x_ref = bf16[16,16,1152]{2,1,0:T(8,128)(2,1)S(1)} custom-call(bf16[4608,64]{1,0:T(8,128)(2,1)S(1)} %bitcast.14), custom_call_target="tpu_custom_call" | custom-call | tf_op jit(solution)/shard_map/pallas_call | solution.py:184
  2.9 0.0 copy-start.1
  2.9 0.0 copy-start.2
  2.9 18.2 %shard_map.56 = bf16[16,16,1152]{2,1,0:T(8,128)(2,1)S(1)} custom-call(bf16[16,16,1152]{2,1,0:T(8,128)(2,1)S(1)} %shard_map.55.x_ref), custom_call_target="tpu_custom_call" | custom-call | tf_op jit(solution)/shard_map/pallas_call | solution.py:190
  21.1 2.0 %collective-permute-start.1 = (bf16[256,1152]{1,0:T(8,128)(2,1)S(1)}, bf16[256,1152]{1,0:T(8,128)(2,1)S(1)}, u32[]{:S(2)}, u32[]{:S(2)}) collective-permute-start(bf16[256,1152]{1,0:T(8,128)(2,1)S(1)} %bitcast.10), channel_id=1, source_target_pairs={{2,0},{4,2},{6,4},{8,6},{10,8},{12,10},{14,12},{16,14},{18,16},{20... | collective-permute-start | bytes 1769480 | tf_op jit(solution)/shard_map/ppermute | solution.py:207
  23.1 4.5 %collective-permute-start = (bf16[256,1152]{1,0:T(8,128)(2,1)S(1)}, bf16[256,1152]{1,0:T(8,128)(2,1)S(1)}, u32[]{:S(2)}, u32[]{:S(2)}) collective-permute-start(bf16[256,1152]{1,0:T(8,128)(2,1)S(1)} %bitcast.11), channel_id=1, source_target_pairs={{0,2},{2,4},{4,6},{6,8},{8,10},{10,12},{12,14},{14,16},{16,18},{18... | collective-permute-start | bytes 1769480 | tf_op jit(solution)/shard_map/ppermute | solution.py:206
  27.6 0.0 copy-done.4
  27.6 0.1 copy.6
  27.7 0.1 rev.3
  27.8 0.0 copy-done.3
  27.8 0.3 copy.8
  28.1 0.1 pad.9.clone
  28.1 5.2 %collective-permute-done.1.right_ref = bf16[256,1152]{1,0:T(8,128)(2,1)S(1)} collective-permute-done((bf16[256,1152]{1,0:T(8,128)(2,1)S(1)}, bf16[256,1152]{1,0:T(8,128)(2,1)S(1)}, u32[]{:S(2)}, u32[]{:S(2)}) %collective-permute-start.1) | collective-permute-done | bytes 589856 | tf_op jit(solution)/shard_map/ppermute | solution.py:207
  33.3 1.1 %collective-permute-done.left_ref = bf16[256,1152]{1,0:T(8,128)(2,1)S(1)} collective-permute-done((bf16[256,1152]{1,0:T(8,128)(2,1)S(1)}, bf16[256,1152]{1,0:T(8,128)(2,1)S(1)}, u32[]{:S(2)}, u32[]{:S(2)}) %collective-permute-start) | collective-permute-done | bytes 589856 | tf_op jit(solution)/shard_map/ppermute | solution.py:206
  34.4 0.0 copy-done.1
  34.4 0.0 copy-done.2
  34.4 21.2 %shard_map.57 = bf16[256,1152]{1,0:T(8,128)(2,1)S(1)} custom-call(s32[1,64]{1,0:T(1,128)S(1)} %copy-done.1, s32[1,64]{1,0:T(1,128)S(1)} %copy-done.2, bf16[256,1152]{1,0:T(8,128)(2,1)S(1)} %collective-permute-done.left_ref, bf16[256,1152]{1,0:T(8,128)(2,1)S(1)} %bitcast.12, bf16[256,1152]{1,0:T(8,128)(2,1)S(1)} %collective-permute-done.1.right_ref, ...), custom_call_target="tpu_custom_call" | custom-call | tf_op jit(solution)/shard_map/pallas_call | solution.py:212
  55.6 23.6 %shard_map.58.landed = bf16[16,16,1152]{2,1,0:T(8,128)(2,1)S(1)} custom-call(bf16[16,16,1152]{2,1,0:T(8,128)(2,1)S(1)} %bitcast.13), custom_call_target="tpu_custom_call" | custom-call | tf_op jit(solution)/shard_map/pallas_call | solution.py:190
  79.2 2.7 %shard_map.59 = bf16[4608,64]{1,0:T(8,128)(2,1)} custom-call(bf16[16,16,1152]{2,1,0:T(8,128)(2,1)S(1)} %shard_map.58.landed), custom_call_target="tpu_custom_call" | custom-call | tf_op jit(solution)/shard_map/pallas_call | solution.py:226
  (1 shorter events, 0.0 us)
Async XLA Ops:
  0.0 1.3 %copy-start = (bf16[2,12,12,16,64]{4,3,2,1,0:T(8,128)(2,1)S(1)}, bf16[2,12,12,16,64]{4,3,2,1,0:T(8,128)(2,1)}, u32[]{:S(2)}) copy-start(bf16[2,12,12,16,64]{4,3,2,1,0:T(8,128)(2,1)} %param.5) | copy-start | bytes 1769476
  1.3 26.3 %copy-start.4 = (f32[9,1,64]{2,1,0:T(1,128)S(1)}, f32[9,1,64]{2,1,0:T(1,128)}, u32[]{:S(2)}) copy-start(f32[9,1,64]{2,1,0:T(1,128)} %param.7) | copy-start | bytes 6916
  1.3 26.5 %copy-start.3 = (bf16[12,12,1,64]{3,1,2,0:T(8,128)(2,1)S(1)}, bf16[12,12,1,64]{3,1,2,0:T(8,128)(2,1)}, u32[]{:S(2)}) copy-start(bf16[12,12,1,64]{3,1,2,0:T(8,128)(2,1)} %param.6) | copy-start | bytes 55300
  2.9 31.6 %copy-start.1 = (s32[1,64]{1,0:T(1,128)S(1)}, s32[1,64]{1,0:T(1,128)}, u32[]{:S(2)}) copy-start(s32[1,64]{1,0:T(1,128)} %near_ref.1) | copy-start | bytes 772
  2.9 31.5 %copy-start.2 = (s32[1,64]{1,0:T(1,128)S(1)}, s32[1,64]{1,0:T(1,128)}, u32[]{:S(2)}) copy-start(s32[1,64]{1,0:T(1,128)} %shift_ref.1) | copy-start | bytes 772
  21.1 12.2 %collective-permute-start.1 = (bf16[256,1152]{1,0:T(8,128)(2,1)S(1)}, bf16[256,1152]{1,0:T(8,128)(2,1)S(1)}, u32[]{:S(2)}, u32[]{:S(2)}) collective-permute-start(bf16[256,1152]{1,0:T(8,128)(2,1)S(1)} %bitcast.10), channel_id=1, source_target_pairs={{2,0},{4,2},{6,4},{8,6},{10,8},{12,10},{14,12},{16,14},{18,16},{20... | collective-permute-start | bytes 1769480 | tf_op jit(solution)/shard_map/ppermute | solution.py:207
  23.1 11.4 %collective-permute-start = (bf16[256,1152]{1,0:T(8,128)(2,1)S(1)}, bf16[256,1152]{1,0:T(8,128)(2,1)S(1)}, u32[]{:S(2)}, u32[]{:S(2)}) collective-permute-start(bf16[256,1152]{1,0:T(8,128)(2,1)S(1)} %bitcast.11), channel_id=1, source_target_pairs={{0,2},{2,4},{4,6},{6,8},{8,10},{10,12},{12,14},{14,16},{16,18},{18... | collective-permute-start | bytes 1769480 | tf_op jit(solution)/shard_map/ppermute | solution.py:206

commit v2 on v1

--- a/solution.py
+++ b/solution.py
@@ -133,7 +133,7 @@
     sub = lax.broadcasted_iota(jnp.int32, (8, energies), 0)
 
     def atom(a, carry):
-        total[...] = jnp.zeros_like(total)
+        held = [None, None]
         for k in range(NBR):
             index = a * NBR + k
             row = weight_ref[pl.ds(index, 1), :]
@@ -158,7 +158,13 @@
             both = (left * right).astype(jnp.bfloat16)
             for c in range(2):
                 part = slice(c * PAIR, (c + 1) * PAIR)
-                total[part, :] += jnp.dot(both, banded[part], preferred_element_type=jnp.float32)
+                term = jnp.dot(both, banded[part], preferred_element_type=jnp.float32)
+                if k % 2 == 0:
+                    held[c] = term
+                elif k == 1:
+                    total[part, :] = held[c] + term
+                else:
+                    total[part, :] += held[c] + term
         return carry
 
     for a in range(per_dev):

time: 82.2 us -> 77.6 us (0.944)
  Pallas kernels: 67.3 us -> 62.7 us
    pallas_call x1, Pallas kernels: 21.2 us -> 16.6 us  [on_device(): pl.pallas_call(scatter_kernel, out_shape=jax.ShapeDtypeStruct((energies,...]
where the time goes in v2:
time: 77.6 us; the launch traced here: 77.4 us
  Pallas kernels  62.7 us (81%)
  starting transfers between devices  6.46 us (8%)
  waiting for transfers between devices  6.29 us (8%)
  local copies, waits for them, and re-layouts  1.82 us (2%)
    pallas_call x2, Pallas kernels, exchanged(): pl.pallas_call(functools.partial(gather_kernel, groups), out_shape=blocks...  41.8 us
    pallas_call x1, Pallas kernels, on_device(): pl.pallas_call(scatter_kernel, out_shape=jax.ShapeDtypeStruct((energies,...  16.6 us
    ppermute x1, waiting for transfers between devices, on_device(): right = lax.ppermute(own, ('energy', 'slab'), [(j, i) for i, j in up])  5.16 us
    ppermute x1, starting transfers between devices, on_device(): left = lax.ppermute(own, ('energy', 'slab'), up)  4.49 us
    pallas_call x1, Pallas kernels, on_device(): pl.pallas_call(functools.partial(unpack_kernel, groups, per_dev), out_sha...  2.74 us
    ppermute x1, starting transfers between devices, on_device(): right = lax.ppermute(own, ('energy', 'slab'), [(j, i) for i, j in up])  1.97 us
    unnamed x12, local copies, waits for them, and re-layouts  1.67 us
    pallas_call x1, Pallas kernels, on_device(): pl.pallas_call(functools.partial(pack_kernel, groups, per_dev), out_shape...  1.59 us
  transfers between devices with their start and end apart: 2, of which 2 were waited for; matrix products, arithmetic and copies ran while one was open for 1% of the time, Pallas kernels for 0%

profile of v2, /device:TPU:15, one launch (start us, length us, event | category | flops | bytes accessed | tf_op | source)
XLA Modules:
  0.0 77.4 jit_solution(13929006524839172725)
XLA Ops:
  0.0 0.0 copy-start
  0.0 1.3 %copy-done = bf16[2,12,12,16,64]{4,3,2,1,0:T(8,128)(2,1)S(1)} copy-done((bf16[2,12,12,16,64]{4,3,2,1,0:T(8,128)(2,1)S(1)}, bf16[2,12,12,16,64]{4,3,2,1,0:T(8,128)(2,1)}, u32[]{:S(2)}) %copy-start) | copy-done | bytes 589848
  1.3 0.0 copy-start.4
  1.3 0.0 copy-start.3
  1.3 1.6 %shard_map.55.x_ref = bf16[16,16,1152]{2,1,0:T(8,128)(2,1)S(1)} custom-call(bf16[4608,64]{1,0:T(8,128)(2,1)S(1)} %bitcast.14), custom_call_target="tpu_custom_call" | custom-call | tf_op jit(solution)/shard_map/pallas_call | solution.py:190
  2.9 0.0 copy-start.1
  2.9 0.0 copy-start.2
  2.9 18.2 %shard_map.56 = bf16[16,16,1152]{2,1,0:T(8,128)(2,1)S(1)} custom-call(bf16[16,16,1152]{2,1,0:T(8,128)(2,1)S(1)} %shard_map.55.x_ref), custom_call_target="tpu_custom_call" | custom-call | tf_op jit(solution)/shard_map/pallas_call | solution.py:196
  21.1 2.0 %collective-permute-start.1 = (bf16[256,1152]{1,0:T(8,128)(2,1)S(1)}, bf16[256,1152]{1,0:T(8,128)(2,1)S(1)}, u32[]{:S(2)}, u32[]{:S(2)}) collective-permute-start(bf16[256,1152]{1,0:T(8,128)(2,1)S(1)} %bitcast.10), channel_id=1, source_target_pairs={{2,0},{4,2},{6,4},{8,6},{10,8},{12,10},{14,12},{16,14},{18,16},{20... | collective-permute-start | bytes 1769480 | tf_op jit(solution)/shard_map/ppermute | solution.py:213
  23.1 4.5 %collective-permute-start = (bf16[256,1152]{1,0:T(8,128)(2,1)S(1)}, bf16[256,1152]{1,0:T(8,128)(2,1)S(1)}, u32[]{:S(2)}, u32[]{:S(2)}) collective-permute-start(bf16[256,1152]{1,0:T(8,128)(2,1)S(1)} %bitcast.11), channel_id=1, source_target_pairs={{0,2},{2,4},{4,6},{6,8},{8,10},{10,12},{12,14},{14,16},{16,18},{18... | collective-permute-start | bytes 1769480 | tf_op jit(solution)/shard_map/ppermute | solution.py:212
  27.6 0.0 copy-done.4
  27.6 0.1 copy.6
  27.7 0.1 rev.3
  27.8 0.0 copy-done.3
  27.8 0.3 copy.8
  28.1 0.1 pad.9.clone
  28.1 5.2 %collective-permute-done.1.right_ref = bf16[256,1152]{1,0:T(8,128)(2,1)S(1)} collective-permute-done((bf16[256,1152]{1,0:T(8,128)(2,1)S(1)}, bf16[256,1152]{1,0:T(8,128)(2,1)S(1)}, u32[]{:S(2)}, u32[]{:S(2)}) %collective-permute-start.1) | collective-permute-done | bytes 589856 | tf_op jit(solution)/shard_map/ppermute | solution.py:213
  33.3 1.1 %collective-permute-done.left_ref = bf16[256,1152]{1,0:T(8,128)(2,1)S(1)} collective-permute-done((bf16[256,1152]{1,0:T(8,128)(2,1)S(1)}, bf16[256,1152]{1,0:T(8,128)(2,1)S(1)}, u32[]{:S(2)}, u32[]{:S(2)}) %collective-permute-start) | collective-permute-done | bytes 589856 | tf_op jit(solution)/shard_map/ppermute | solution.py:212
  34.4 0.0 copy-done.1
  34.4 0.0 copy-done.2
  34.4 16.6 %shard_map.57 = bf16[256,1152]{1,0:T(8,128)(2,1)S(1)} custom-call(s32[1,64]{1,0:T(1,128)S(1)} %copy-done.1, s32[1,64]{1,0:T(1,128)S(1)} %copy-done.2, bf16[256,1152]{1,0:T(8,128)(2,1)S(1)} %collective-permute-done.left_ref, bf16[256,1152]{1,0:T(8,128)(2,1)S(1)} %bitcast.12, bf16[256,1152]{1,0:T(8,128)(2,1)S(1)} %collective-permute-done.1.right_ref, ...), custom_call_target="tpu_custom_call" | custom-call | tf_op jit(solution)/shard_map/pallas_call | solution.py:218
  51.0 23.6 %shard_map.58.landed = bf16[16,16,1152]{2,1,0:T(8,128)(2,1)S(1)} custom-call(bf16[16,16,1152]{2,1,0:T(8,128)(2,1)S(1)} %bitcast.13), custom_call_target="tpu_custom_call" | custom-call | tf_op jit(solution)/shard_map/pallas_call | solution.py:196
  74.6 2.7 %shard_map.59 = bf16[4608,64]{1,0:T(8,128)(2,1)} custom-call(bf16[16,16,1152]{2,1,0:T(8,128)(2,1)S(1)} %shard_map.58.landed), custom_call_target="tpu_custom_call" | custom-call | tf_op jit(solution)/shard_map/pallas_call | solution.py:232
  (1 shorter events, 0.0 us)
Async XLA Ops:
  0.0 1.3 %copy-start = (bf16[2,12,12,16,64]{4,3,2,1,0:T(8,128)(2,1)S(1)}, bf16[2,12,12,16,64]{4,3,2,1,0:T(8,128)(2,1)}, u32[]{:S(2)}) copy-start(bf16[2,12,12,16,64]{4,3,2,1,0:T(8,128)(2,1)} %param.5) | copy-start | bytes 1769476
  1.3 26.3 %copy-start.4 = (f32[9,1,64]{2,1,0:T(1,128)S(1)}, f32[9,1,64]{2,1,0:T(1,128)}, u32[]{:S(2)}) copy-start(f32[9,1,64]{2,1,0:T(1,128)} %param.7) | copy-start | bytes 6916
  1.3 26.5 %copy-start.3 = (bf16[12,12,1,64]{3,1,2,0:T(8,128)(2,1)S(1)}, bf16[12,12,1,64]{3,1,2,0:T(8,128)(2,1)}, u32[]{:S(2)}) copy-start(bf16[12,12,1,64]{3,1,2,0:T(8,128)(2,1)} %param.6) | copy-start | bytes 55300
  2.9 31.6 %copy-start.1 = (s32[1,64]{1,0:T(1,128)S(1)}, s32[1,64]{1,0:T(1,128)}, u32[]{:S(2)}) copy-start(s32[1,64]{1,0:T(1,128)} %near_ref.1) | copy-start | bytes 772
  2.9 31.5 %copy-start.2 = (s32[1,64]{1,0:T(1,128)S(1)}, s32[1,64]{1,0:T(1,128)}, u32[]{:S(2)}) copy-start(s32[1,64]{1,0:T(1,128)} %shift_ref.1) | copy-start | bytes 772
  21.1 12.2 %collective-permute-start.1 = (bf16[256,1152]{1,0:T(8,128)(2,1)S(1)}, bf16[256,1152]{1,0:T(8,128)(2,1)S(1)}, u32[]{:S(2)}, u32[]{:S(2)}) collective-permute-start(bf16[256,1152]{1,0:T(8,128)(2,1)S(1)} %bitcast.10), channel_id=1, source_target_pairs={{2,0},{4,2},{6,4},{8,6},{10,8},{12,10},{14,12},{16,14},{18,16},{20... | collective-permute-start | bytes 1769480 | tf_op jit(solution)/shard_map/ppermute | solution.py:213
  23.1 11.4 %collective-permute-start = (bf16[256,1152]{1,0:T(8,128)(2,1)S(1)}, bf16[256,1152]{1,0:T(8,128)(2,1)S(1)}, u32[]{:S(2)}, u32[]{:S(2)}) collective-permute-start(bf16[256,1152]{1,0:T(8,128)(2,1)S(1)} %bitcast.11), channel_id=1, source_target_pairs={{0,2},{2,4},{4,6},{6,8},{8,10},{10,12},{12,14},{14,16},{16,18},{18... | collective-permute-start | bytes 1769480 | tf_op jit(solution)/shard_map/ppermute | solution.py:212
